TPU v7x, 32 devices: a whole 2x2x4 slice. The times are simulated.
32 devices in a mesh: grp: 2 (over y), gx: 4 (over z), gy: 2 (over x), gz: 2 (over core).
Axes of the slice: x: 2, y: 2, z: 4, core: 2. Of those that a mesh axis runs over, the one named last changes fastest.
Arguments:
- parcel_values: bfloat16 [6, 131072], P(None, ('grp', 'gx', 'gy', 'gz')), parts along dimension 1, may hold values from -2304 to 2304
- parcel_owner: int32 [131072, 1], P(('grp', 'gx', 'gy', 'gz')), parts along dimension 0, may hold values from 0 to 3; in each aligned block of 4096 rows (0 to 4095, 4096 to 8191, ...) at most 1536 rows name the same one
- parcel_cell: int32 [131072], P(('grp', 'gx', 'gy', 'gz')), parts along dimension 0, may hold values from 0 to 65535
- live_counts: int32 [32], P(('grp', 'gx', 'gy', 'gz')), parts along dimension 0, may hold values from 1 to 4096, 49152 in all
- fluid_state: bfloat16 [6, 256, 32, 256], P(None, ('grp', 'gx'), 'gy', 'gz'), parts along dimension 1, may hold values from -6 to 6
Outputs:
- coupled: bfloat16 [6, 256, 32, 256], P(None, ('grp', 'gx'), 'gy', 'gz'), parts along dimension 1
There are 2 independent parts, one for each index of `grp`. A program takes and returns all parts, laid end to end along the dimension named above; each array names one. Nothing has to cross between parts.
Inputs may be any that keep to these rules, and one draw needn't show every extreme that they name: `parcel_owner`: among the rows of one brick no streamwise index is named by more than 1536 rows; some brick names one exactly 1536 times. `parcel_cell`: cells are numbered (x * 16 + y) * 128 + z within the brick. `live_counts`: A brick's live parcels are its first rows; some brick has all rows live.
All inputs are finite; a program needn't handle non-finite values. No bound on the sum of `live_counts` on one device may be relied on, other than what follows from the above.
Results may differ from a plain program's by a relative error of at most 0.005.
Values may be sent and summed in bfloat16 or wider, within the bound.
A program may use at most 64 MiB of HBM per device.

v0:
```python
import jax
import jax.numpy as jnp
from jax import lax
from jax.sharding import PartitionSpec as P

REACH = 16
spread_cells = 12.0


def padded(shard, sides, width):
    for axis, dim in sides:
        size, length = (lax.axis_size(axis), shard.shape[dim])
        up = [(i, (i + 1) % size) for i in range(size)]
        down = [(j, i) for i, j in up]
        last = lax.slice_in_dim(shard, length - width, length, axis=dim)
        initial = lax.slice_in_dim(shard, 0, width, axis=dim)
        before = lax.ppermute(last, axis, up)
        after = lax.ppermute(initial, axis, down)
        shard = jnp.concatenate([before, shard, after], axis=dim)
    return shard


def tap_curve(offsets):
    tap_grid = jnp.arange(2 * REACH + 1).astype(jnp.float32)
    tap_sum = jnp.sum(
        jnp.exp(-(tap_grid - REACH) * (tap_grid - REACH) / (2.0 * spread_cells * spread_cells))
    )
    return (
        jnp.exp(-(offsets - REACH) * (offsets - REACH) / (2.0 * spread_cells * spread_cells))
        / tap_sum
    )


def banded(out_rows, in_rows, shift):
    row_ids = lax.broadcasted_iota(jnp.int32, (out_rows, in_rows), 0)
    col_ids = lax.broadcasted_iota(jnp.int32, (out_rows, in_rows), 1)
    offset_ids = col_ids - row_ids + shift
    inside = (offset_ids >= 0) & (offset_ids <= 2 * REACH)
    values = tap_curve(offset_ids.astype(jnp.float32)).astype(jnp.bfloat16)
    return jnp.where(inside, values, jnp.zeros_like(values))


def on_device(parcel_values, parcel_owner, parcel_cell, live_counts, fluid_state):
    channels, count_dev = parcel_values.shape
    width_x, width_y, width_z = (fluid_state.shape[1], fluid_state.shape[2], fluid_state.shape[3])
    owners = lax.axis_size("gx")
    capacity = 3 * count_dev // (2 * owners)
    owner_ids = parcel_owner[:, 0]
    local_rows = jnp.arange(count_dev, dtype=jnp.int32)
    is_live = local_rows < live_counts[0]
    owner_hits = (
        (owner_ids[:, None] == jnp.arange(owners, dtype=jnp.int32)[None, :]) & is_live[:, None]
    ).astype(jnp.int32)
    position = jnp.sum(jnp.cumsum(owner_hits, axis=0) * owner_hits, axis=1) - 1
    slot_index = jnp.where(is_live, owner_ids * capacity + position, owners * capacity)
    cell_xpart = (parcel_cell // (width_y * width_z)).astype(jnp.bfloat16)
    cell_ypart = (parcel_cell // width_z % width_y).astype(jnp.bfloat16)
    cell_low = (parcel_cell % width_z).astype(jnp.bfloat16)
    send_rows = jnp.concatenate(
        [parcel_values, cell_xpart[None, :], cell_ypart[None, :], cell_low[None, :]], axis=0
    )
    packed = (
        jnp.zeros((channels + 3, owners * capacity), jnp.bfloat16)
        .at[:, slot_index]
        .set(send_rows, mode="drop")
    )
    packed = packed.reshape(channels + 3, owners, capacity)
    arrived = lax.all_to_all(packed, "gx", split_axis=1, concat_axis=1, tiled=True).reshape(
        channels + 3, owners * capacity
    )
    slot_total = owners * capacity
    block_rows = min(1024, slot_total)
    plane_cells = width_x * width_y
    high_grid = jnp.arange(plane_cells, dtype=jnp.float32)
    low_grid = jnp.arange(width_z, dtype=jnp.float32)

    def deposit(step_index, summed):
        window = lax.dynamic_slice_in_dim(arrived, step_index * block_rows, block_rows, 1)
        high_ids = window[channels].astype(jnp.float32) * width_y + window[channels + 1].astype(
            jnp.float32
        )
        high_hot = (high_ids[:, None] == high_grid[None, :]).astype(jnp.bfloat16)
        low_hot = (window[channels + 2].astype(jnp.float32)[:, None] == low_grid[None, :]).astype(
            jnp.bfloat16
        )
        weighted = window[:channels][:, :, None] * low_hot[None, :, :]
        return summed + jnp.einsum(
            "sh,csz->chz", high_hot, weighted, preferred_element_type=jnp.float32
        )

    summed = lax.fori_loop(
        0,
        slot_total // block_rows,
        deposit,
        jnp.zeros((channels, plane_cells, width_z), jnp.float32),
    )
    source = summed.reshape(channels, width_x, width_y, width_z).astype(jnp.bfloat16)
    flat_source = source.reshape(channels, width_x, width_y * width_z)
    pencil = lax.all_to_all(flat_source, "gx", split_axis=2, concat_axis=1, tiled=True)
    full_x = pencil.shape[1]
    smoothed = jnp.einsum(
        "ij,cjk->cik", banded(full_x, full_x, REACH), pencil, preferred_element_type=jnp.float32
    ).astype(jnp.bfloat16)
    after_x = lax.all_to_all(smoothed, "gx", split_axis=1, concat_axis=2, tiled=True)
    after_x = after_x.reshape(channels, width_x, width_y, width_z)
    extended_y = padded(after_x, (("gy", 2),), REACH)
    after_y = jnp.einsum(
        "ij,cxjz->cxiz",
        banded(width_y, width_y + 2 * REACH, 0),
        extended_y,
        preferred_element_type=jnp.float32,
    ).astype(jnp.bfloat16)
    extended_z = padded(after_y, (("gz", 3),), REACH)
    smooth_z = jnp.einsum(
        "cxyj,ij->cxyi",
        extended_z,
        banded(width_z, width_z + 2 * REACH, 0),
        preferred_element_type=jnp.float32,
    )
    return (fluid_state.astype(jnp.float32) + smooth_z).astype(jnp.bfloat16)


def solution(mesh):
    in_specs = (
        P(None, ("grp", "gx", "gy", "gz")),
        P(("grp", "gx", "gy", "gz"), None),
        P(("grp", "gx", "gy", "gz")),
        P(("grp", "gx", "gy", "gz")),
        P(None, ("grp", "gx"), "gy", "gz"),
    )
    out_specs = P(None, ("grp", "gx"), "gy", "gz")
    return jax.shard_map(
        on_device, mesh=mesh, in_specs=in_specs, out_specs=out_specs, check_vma=False
    )
```

profile of v0, /device:TPU:0, one launch (start us, length us, event | category | flops | bytes accessed | tf_op | source)
XLA Modules:
  0.0 157.6 jit_solution(1705467644931148753)
XLA Ops:
  0.7 0.7 fusion.61
  1.4 1.2 reduce-window.6
  2.6 0.2 slice_reduce_fusion
  2.8 0.2 reduce-window.9
  3.1 0.8 fusion.53
  3.9 0.8 fusion.79
  4.8 0.9 maximum_bitcast_fusion
  5.7 0.5 copy.30
  6.3 11.4 %scatter_custom_fusion = bf16[9,6144]{0,1:T(8,128)(2,1)S(1)} fusion(s32[4096]{0:T(1024)S(1)} %bitcast.85, bf16[4096,9]{1,0:T(8,128)(2,1)S(1)} %copy.30, bf16[]{:T(256)} %constant.117.clone.1), kind=kCustom, calls=%fused_computation.36 | custom fusion | bytes 110594 | tf_op jit(solution)/shard_map/scatter | solution.py:65
  17.6 1.4 copy.31
  19.0 6.3 %all-to-all-start = ((bf16[9,4,1536]{2,0,1:T(8,128)(2,1)}), bf16[9,4,1536]{2,0,1:T(8,128)(2,1)S(1)}, u32[]{:S(2)}, u32[]{:S(2)}) async-start(bf16[9,4,1536]{2,0,1:T(8,128)(2,1)} %copy.31), calls=%async_computation | async-start | bytes 393216 | tf_op jit(solution)/shard_map/all_to_all | solution.py:68
  25.3 7.5 %all-to-all-done = bf16[9,4,1536]{2,0,1:T(8,128)(2,1)S(1)} async-done(((bf16[9,4,1536]{2,0,1:T(8,128)(2,1)}), bf16[9,4,1536]{2,0,1:T(8,128)(2,1)S(1)}, u32[]{:S(2)}, u32[]{:S(2)}) %all-to-all-start) | async-done | bytes 110624 | tf_op jit(solution)/shard_map/all_to_all | solution.py:68
  33.1 9.3 %while.14 = (s32[]{:T(128)}, f32[6,512,128]{1,2,0:T(8,128)S(1)}, bf16[9,6144]{1,0:T(8,128)(2,1)S(1)}, s32[]{:T(128)}, s32[]{:T(128)}, /*index=5*/s32[]{}, s32[]{:T(128)}, s32[]{:T(128)}, s32[]{}, s32[]{}) while((s32[]{:T(128)}, f32[6,512,128]{1,2,0:T(8,128)S(1)}, bf16[9,6144]{1,0:T(8,128)(2,1)S(1)}, s32[]{:T(128)}, s32[]{:T(128)}, ...), condition=%wide.region_5.6_spmd.clone, body=%wide.region_4.5_spmd.clone.sunk | while | flops 807670784 | bytes 3729625 | solution.py:91
  33.3 1.3 bitcast_add_fusion.2
  34.8 1.3 bitcast_add_fusion.2
  36.4 1.3 bitcast_add_fusion.2
  37.9 1.3 bitcast_add_fusion.2
  39.5 1.3 bitcast_add_fusion.2
  41.0 1.3 bitcast_add_fusion.2
  42.5 0.4 copy.33
  42.8 0.3 convert_element_type.120
  43.2 4.2 %copy.34 = bf16[6,32,2048]{1,0,2:T(8,128)(2,1)} copy(bf16[6,32,2048]{2,1,0:T(8,128)(2,1)S(1)} %convert_element_type.120) | data formatting | bytes 1572864 | tf_op jit(solution)/shard_map/convert_element_type | solution.py:97
  47.4 5.7 %reshape.138 = bf16[4,2,49152]{2,1,0:T(2,128)(2,1)} reshape(bf16[2048,6,32]{2,1,0:T(8,128)(2,1)} %bitcast.72) | data formatting | bytes 1572864
  53.1 3.5 %all-to-all-start.1 = ((bf16[4,2,49152]{2,1,0:T(2,128)(2,1)}), bf16[4,2,49152]{2,1,0:T(2,128)(2,1)S(1)}, u32[]{:S(2)}, u32[]{:S(2)}) async-start(bf16[4,2,49152]{2,1,0:T(2,128)(2,1)} %reshape.138), calls=%async_computation.1 | async-start | bytes 1572864 | tf_op jit(solution)/shard_map/all_to_all | solution.py:99
  56.6 0.6 fusion.104
  57.2 18.1 %all-to-all-done.1 = bf16[4,2,49152]{2,1,0:T(2,128)(2,1)S(1)} async-done(((bf16[4,2,49152]{2,1,0:T(2,128)(2,1)}), bf16[4,2,49152]{2,1,0:T(2,128)(2,1)S(1)}, u32[]{:S(2)}, u32[]{:S(2)}) %all-to-all-start.1) | async-done | bytes 786464 | tf_op jit(solution)/shard_map/all_to_all | solution.py:99
  75.3 4.2 %reshape.139 = bf16[2048,6,32]{2,1,0:T(8,128)(2,1)} reshape(bf16[4,2,49152]{2,1,0:T(2,128)(2,1)S(1)} %all-to-all-done.1) | data formatting | bytes 1572864
  79.5 4.5 %copy.48 = bf16[6,32,4,512]{3,2,1,0:T(4,128)(2,1)S(1)} copy(bf16[6,32,4,512]{1,0,3,2:T(8,128)(2,1)} %bitcast.73) | data formatting | bytes 1572864 | tf_op jit(solution)/shard_map/all_to_all | solution.py:99
  84.0 0.2 copy.36
  84.2 1.0 fusion.38
  85.2 0.9 copy.38
  86.1 27.7 %all_to_all.38 = bf16[6,128,512]{2,0,1:T(8,128)(2,1)S(1)} all-to-all(bf16[6,128,512]{2,0,1:T(8,128)(2,1)S(1)} %copy.38), channel_id=1, replica_groups=mesh['grp'=2,'gx'=4,'gy'=2,'gz'=2] {'gx'}, dimensions={1} | all-to-all | bytes 1572864 | tf_op jit(solution)/shard_map/all_to_all | solution.py:104
  113.8 0.6 copy.40
  114.4 0.3 reshape.120
  114.7 1.6 collective-permute-start
  116.2 0.5 collective-permute-start.1
  116.8 18.5 %collective-permute-done = bf16[6,32,16,128]{3,2,1,0:T(8,128)(2,1)S(1)} collective-permute-done((bf16[6,32,16,128]{3,2,1,0:T(8,128)(2,1)S(1)}, bf16[6,32,16,128]{3,2,1,0:T(8,128)(2,1)S(1)}, u32[]{:S(2)}, u32[]{:S(2)}) %collective-permute-start) | collective-permute-done | bytes 786464 | tf_op jit(solution)/shard_map/ppermute | solution.py:17
  135.2 14.4 %collective-permute-done.1 = bf16[6,32,16,128]{3,2,1,0:T(8,128)(2,1)S(1)} collective-permute-done((bf16[6,32,16,128]{3,2,1,0:T(8,128)(2,1)S(1)}, bf16[6,32,16,128]{3,2,1,0:T(8,128)(2,1)S(1)}, u32[]{:S(2)}, u32[]{:S(2)}) %collective-permute-start.1) | collective-permute-done | bytes 786464 | tf_op jit(solution)/shard_map/ppermute | solution.py:18
  149.7 1.1 fusion.35
  150.7 0.4 fusion.123
  151.1 0.6 copy.41
  151.8 0.6 copy.42
  152.5 0.5 collective-permute-start.3
  153.0 0.5 collective-permute-done.2
  153.5 0.6 copy.43
  154.2 0.2 collective-permute-done.3
  154.3 0.6 copy.44
  155.0 2.6 %add_convert_fusion = bf16[6,32,16,128]{3,2,1,0:T(8,128)(2,1)} fusion(bf16[6,32,16,128]{3,2,1,0:T(8,128)(2,1)S(1)} %copy-done.1, bf16[6,32,16,16]{3,2,1,0:T(8,128)(2,1)S(1)} %copy.44, bf16[6,32,16,128]{3,2,1,0:T(8,128)(2,1)S(1)} %fusion.35, bf16[6,32,16,16]{3,2,1,0:T(8,128)(2,1)S(1)} %copy.43, f32[]{:T(128)} %fusion.104), kind=kOutput, calls=%fused_computation.31 | convolution fusion | flops 130203648 | bytes 2555908 | tf_op jit(solution)/shard_map/cxyj,ij->cxyi/dot_general | solution.py:114
  (42 shorter events, 1.6 us)
Async XLA Ops:
  0.0 6.2 %copy-start = (s32[4096,1]{0,1:T(1,128)S(1)}, s32[4096,1]{0,1:T(1,128)}, u32[]{:S(2)}) copy-start(s32[4096,1]{0,1:T(1,128)} %param.8) | copy-start | bytes 49156
  19.0 13.8 %all-to-all-start = ((bf16[9,4,1536]{2,0,1:T(8,128)(2,1)}), bf16[9,4,1536]{2,0,1:T(8,128)(2,1)S(1)}, u32[]{:S(2)}, u32[]{:S(2)}) async-start(bf16[9,4,1536]{2,0,1:T(8,128)(2,1)} %copy.31), calls=%async_computation | async-start | bytes 393216 | tf_op jit(solution)/shard_map/all_to_all | solution.py:68
  53.1 22.2 %all-to-all-start.1 = ((bf16[4,2,49152]{2,1,0:T(2,128)(2,1)}), bf16[4,2,49152]{2,1,0:T(2,128)(2,1)S(1)}, u32[]{:S(2)}, u32[]{:S(2)}) async-start(bf16[4,2,49152]{2,1,0:T(2,128)(2,1)} %reshape.138), calls=%async_computation.1 | async-start | bytes 1572864 | tf_op jit(solution)/shard_map/all_to_all | solution.py:99
  114.7 20.5 %collective-permute-start = (bf16[6,32,16,128]{3,2,1,0:T(8,128)(2,1)S(1)}, bf16[6,32,16,128]{3,2,1,0:T(8,128)(2,1)S(1)}, u32[]{:S(2)}, u32[]{:S(2)}) collective-permute-start(bf16[6,32,16,128]{3,2,1,0:T(8,128)(2,1)S(1)} %reshape.120), channel_id=1, source_target_pairs={{0,2},{2,0},{1,3},{3,1},{4,6},{6,4},{5,7},{7,5},{8,10},{10,8},{9,1... | collective-permute-start | bytes 2359304 | tf_op jit(solution)/shard_map/ppermute | solution.py:17
  116.2 33.4 %collective-permute-start.1 = (bf16[6,32,16,128]{3,2,1,0:T(8,128)(2,1)S(1)}, bf16[6,32,16,128]{3,2,1,0:T(8,128)(2,1)S(1)}, u32[]{:S(2)}, u32[]{:S(2)}) collective-permute-start(bf16[6,32,16,128]{3,2,1,0:T(8,128)(2,1)S(1)} %reshape.120), channel_id=1, source_target_pairs={{2,0},{0,2},{3,1},{1,3},{6,4},{4,6},{7,5},{5,7},{10,8},{8,10},{11,... | collective-permute-start | bytes 2359304 | tf_op jit(solution)/shard_map/ppermute | solution.py:18
  151.7 1.8 %collective-permute-start.2 = (bf16[6,32,16,16]{1,3,2,0:T(8,128)(2,1)S(1)}, bf16[6,32,16,16]{1,3,2,0:T(8,128)(2,1)S(1)}, u32[]{:S(2)}, u32[]{:S(2)}) collective-permute-start(bf16[6,32,16,16]{1,3,2,0:T(8,128)(2,1)S(1)} %copy.41), channel_id=1, source_target_pairs={{0,1},{1,0},{2,3},{3,2},{4,5},{5,4},{6,7},{7,6},{8,9},{9,8},{10,11... | collective-permute-start | bytes 294920 | tf_op jit(solution)/shard_map/ppermute | solution.py:17
  151.8 3.2 %copy-start.1 = (bf16[6,32,16,128]{3,2,1,0:T(8,128)(2,1)S(1)}, bf16[6,32,16,128]{3,2,1,0:T(8,128)(2,1)}, u32[]{:S(2)}) copy-start(bf16[6,32,16,128]{3,2,1,0:T(8,128)(2,1)} %param.11) | copy-start | bytes 2359300
  152.5 1.9 %collective-permute-start.3 = (bf16[6,32,16,16]{1,3,2,0:T(8,128)(2,1)S(1)}, bf16[6,32,16,16]{1,3,2,0:T(8,128)(2,1)S(1)}, u32[]{:S(2)}, u32[]{:S(2)}) collective-permute-start(bf16[6,32,16,16]{1,3,2,0:T(8,128)(2,1)S(1)} %copy.42), channel_id=1, source_target_pairs={{1,0},{0,1},{3,2},{2,3},{5,4},{4,5},{7,6},{6,7},{9,8},{8,9},{11,10... | collective-permute-start | bytes 294920 | tf_op jit(solution)/shard_map/ppermute | solution.py:18
where the time goes:
time: 158 us
  waiting for transfers between devices  59.2 us (37%)
  local copies, waits for them, and re-layouts  37.9 us (24%)
  blocking collectives  27.7 us (18%)
  matrix products  12.6 us (8%)
  starting transfers between devices  12.5 us (8%)
  other arithmetic  6.49 us (4%)
    all_to_all x1, blocking collectives, on_device(): lax.all_to_all(smoothed, 'gx', split_axis=1, concat_axis=2, tiled=True)  27.7 us
    ppermute x2, waiting for transfers between devices, padded(): before = lax.ppermute(last, axis, up)  19 us
    all_to_all x1, waiting for transfers between devices, on_device(): lax.all_to_all(flat_source, 'gx', split_axis=2, concat_axis=1, tiled=True)  18.1 us
    ppermute x2, waiting for transfers between devices, padded(): after = lax.ppermute(initial, axis, down)  14.6 us
    scatter x1, local copies, waits for them, and re-layouts, on_device(): packed = jnp.zeros((channels + 3, owners * capacity), jnp.bfloat16).at[:,...  11.4 us
    unnamed x8, local copies, waits for them, and re-layouts  9.98 us
    dot_general x6, matrix products, deposit(): jnp.einsum('sh,csz->chz', high_hot, weighted, preferred_element_type=jnp....  7.91 us
    all_to_all x1, waiting for transfers between devices, on_device(): lax.all_to_all(packed, 'gx', split_axis=1, concat_axis=1, tiled=True)  7.51 us
  transfers between devices with their start and end apart: 6, of which 6 were waited for; matrix products, arithmetic and copies ran while one was open for 1% of the time, Pallas kernels for 0%

commit v1 on v0

--- a/solution.py
+++ b/solution.py
@@ -1,3 +1,4 @@
+import functools
 import jax
 import jax.numpy as jnp
 from jax import lax
@@ -5,6 +6,39 @@
 
 REACH = 16
 spread_cells = 12.0
+
+
+def matrix_render(message, out_dim, field_in):
+    block_out = message.shape
+    parts_out = message.reshape(
+        *block_out[:out_dim], field_in, block_out[out_dim] // field_in, *block_out[out_dim + 1 :]
+    )
+    return jnp.moveaxis(parts_out, out_dim, 0)
+
+
+def order_local_data_on_mesh(incoming_x, dim_k):
+    incoming_x = jnp.moveaxis(incoming_x, 0, dim_k)
+    response = incoming_x.shape
+    return incoming_x.reshape(
+        *response[:dim_k], response[dim_k] * response[dim_k + 1], *response[dim_k + 2 :]
+    )
+
+
+def group_the_stages_all(vector, ax_name, x0, payload):
+    now = lax.psum(1, ax_name)
+    v1 = lax.axis_index(ax_name)
+    z2, side_arr = (now, v1)
+    opened = matrix_render(vector, x0, z2)
+    t_next = opened
+    for k in tuple(range(1, z2)):
+        local_part, tmp = ((side_arr + k) % z2, (side_arr - k) % z2)
+        long_array = lax.dynamic_index_in_dim(opened, local_part, 0)
+        odd = lax.ppermute(long_array, ax_name, [(it, (it + k) % z2) for it in range(z2)])
+        t_next = lax.dynamic_update_slice_in_dim(t_next, odd, tmp, axis=0)
+    return order_local_data_on_mesh(t_next, payload)
+
+
+drive_scales = functools.partial(group_the_stages_all, ax_name="gx", x0=1, payload=2)
 
 
 def padded(shard, sides, width):
@@ -101,7 +135,7 @@
     smoothed = jnp.einsum(
         "ij,cjk->cik", banded(full_x, full_x, REACH), pencil, preferred_element_type=jnp.float32
     ).astype(jnp.bfloat16)
-    after_x = lax.all_to_all(smoothed, "gx", split_axis=1, concat_axis=2, tiled=True)
+    after_x = drive_scales(smoothed)
     after_x = after_x.reshape(channels, width_x, width_y, width_z)
     extended_y = padded(after_x, (("gy", 2),), REACH)
     after_y = jnp.einsum(

time: 158 us -> 148 us (0.937); the launches traced: 158 us -> 145 us
  blocking collectives: 27.7 us -> 0 us
  waiting for transfers between devices: 59.2 us -> 71.1 us
  starting transfers between devices: 12.5 us -> 16.4 us
    all_to_all x1 -> x0, blocking collectives: 27.7 us -> none  [on_device(): lax.all_to_all(smoothed, 'gx', split_axis=1, concat_axis=2, tiled=True)]
    ppermute x0 -> x3, waiting for transfers between devices: none -> 12.4 us  [group_the_stages_all(): lax.ppermute(long_array, ax_name, [(it, (it + k) % z2) for it in range(z2)])]
    ppermute x2, waiting for transfers between devices: 19 us -> 14.2 us  [padded(): before = lax.ppermute(last, axis, up)]
    ppermute x2, waiting for transfers between devices: 14.6 us -> 19 us  [padded(): after = lax.ppermute(initial, axis, down)]
    ppermute x0 -> x3, starting transfers between devices: none -> 3.87 us  [group_the_stages_all(): lax.ppermute(long_array, ax_name, [(it, (it + k) % z2) for it in range(z2)])]
  transfers between devices with their start and end apart: 6 -> 9, of which waited for: 6 -> 8; matrix products, arithmetic and copies ran while one was open for 1% -> 1% of each run, Pallas kernels for 0% -> 0%
where the time goes in v1:
time: 148 us; the launch traced here: 145 us
  waiting for transfers between devices  71.1 us (48%)
  local copies, waits for them, and re-layouts  37.1 us (25%)
  starting transfers between devices  16.4 us (11%)
  matrix products  12.5 us (8%)
  other arithmetic  6.49 us (4%)
    ppermute x2, waiting for transfers between devices, padded(): after = lax.ppermute(initial, axis, down)  19 us
    all_to_all x1, waiting for transfers between devices, on_device(): lax.all_to_all(flat_source, 'gx', split_axis=2, concat_axis=1, tiled=True)  18 us
    ppermute x2, waiting for transfers between devices, padded(): before = lax.ppermute(last, axis, up)  14.2 us
    ppermute x3, waiting for transfers between devices, group_the_stages_all(): lax.ppermute(long_array, ax_name, [(it, (it + k) % z2) for it in range(z2)])  12.4 us
    scatter x1, local copies, waits for them, and re-layouts, on_device(): packed = jnp.zeros((channels + 3, owners * capacity), jnp.bfloat16).at[:,...  11.4 us
    unnamed x8, local copies, waits for them, and re-layouts  9.97 us
    dot_general x6, matrix products, deposit(): jnp.einsum('sh,csz->chz', high_hot, weighted, preferred_element_type=jnp....  7.91 us
    all_to_all x1, waiting for transfers between devices, on_device(): lax.all_to_all(packed, 'gx', split_axis=1, concat_axis=1, tiled=True)  7.51 us
  transfers between devices with their start and end apart: 9, of which 8 were waited for; matrix products, arithmetic and copies ran while one was open for 1% of the time, Pallas kernels for 0%

profile of v1, /device:TPU:0, one launch (start us, length us, event | category | flops | bytes accessed | tf_op | source)
XLA Modules:
  0.0 144.9 jit_solution(562370054770898233)
XLA Ops:
  0.7 0.7 fusion.60
  1.4 1.2 reduce-window.6
  2.6 0.2 slice_reduce_fusion
  2.8 0.2 reduce-window.9
  3.1 0.8 fusion.52
  3.9 0.8 fusion.78
  4.8 0.9 maximum_bitcast_fusion
  5.7 0.5 copy.25
  6.3 11.4 %scatter_custom_fusion = bf16[9,6144]{0,1:T(8,128)(2,1)S(1)} fusion(s32[4096]{0:T(1024)S(1)} %bitcast.94, bf16[4096,9]{1,0:T(8,128)(2,1)S(1)} %copy.25, bf16[]{:T(256)} %constant.164.clone.1), kind=kCustom, calls=%fused_computation.35 | custom fusion | bytes 110594 | tf_op jit(solution)/shard_map/scatter | solution.py:99
  17.6 1.4 copy.26
  19.0 6.3 %all-to-all-start = ((bf16[9,4,1536]{2,0,1:T(8,128)(2,1)}), bf16[9,4,1536]{2,0,1:T(8,128)(2,1)S(1)}, u32[]{:S(2)}, u32[]{:S(2)}) async-start(bf16[9,4,1536]{2,0,1:T(8,128)(2,1)} %copy.26), calls=%async_computation | async-start | bytes 393216 | tf_op jit(solution)/shard_map/all_to_all | solution.py:102
  25.3 7.5 %all-to-all-done = bf16[9,4,1536]{2,0,1:T(8,128)(2,1)S(1)} async-done(((bf16[9,4,1536]{2,0,1:T(8,128)(2,1)}), bf16[9,4,1536]{2,0,1:T(8,128)(2,1)S(1)}, u32[]{:S(2)}, u32[]{:S(2)}) %all-to-all-start) | async-done | bytes 110624 | tf_op jit(solution)/shard_map/all_to_all | solution.py:102
  33.1 9.3 %while.14 = (s32[]{:T(128)}, f32[6,512,128]{1,2,0:T(8,128)S(1)}, bf16[9,6144]{1,0:T(8,128)(2,1)S(1)}, s32[]{:T(128)}, s32[]{:T(128)}, /*index=5*/s32[]{}, s32[]{:T(128)}, s32[]{:T(128)}, s32[]{}, s32[]{}) while((s32[]{:T(128)}, f32[6,512,128]{1,2,0:T(8,128)S(1)}, bf16[9,6144]{1,0:T(8,128)(2,1)S(1)}, s32[]{:T(128)}, s32[]{:T(128)}, ...), condition=%wide.region_5.6_spmd.clone, body=%wide.region_4.5_spmd.clone.sunk | while | flops 807670784 | bytes 3729633 | solution.py:125
  33.3 1.3 bitcast_add_fusion.2
  34.8 1.3 bitcast_add_fusion.2
  36.4 1.3 bitcast_add_fusion.2
  37.9 1.3 bitcast_add_fusion.2
  39.5 1.3 bitcast_add_fusion.2
  41.0 1.3 bitcast_add_fusion.2
  42.5 0.4 copy.28
  42.8 0.3 convert_element_type.120
  43.2 4.2 %copy.29 = bf16[6,32,2048]{1,0,2:T(8,128)(2,1)} copy(bf16[6,32,2048]{2,1,0:T(8,128)(2,1)S(1)} %convert_element_type.120) | data formatting | bytes 1572864 | tf_op jit(solution)/shard_map/convert_element_type | solution.py:131
  47.4 5.7 %reshape.140 = bf16[4,2,49152]{2,1,0:T(2,128)(2,1)} reshape(bf16[2048,6,32]{2,1,0:T(8,128)(2,1)} %bitcast.79) | data formatting | bytes 1572864
  53.1 3.5 %all-to-all-start.1 = ((bf16[4,2,49152]{2,1,0:T(2,128)(2,1)}), bf16[4,2,49152]{2,1,0:T(2,128)(2,1)S(1)}, u32[]{:S(2)}, u32[]{:S(2)}) async-start(bf16[4,2,49152]{2,1,0:T(2,128)(2,1)} %reshape.140), calls=%async_computation.1 | async-start | bytes 1572864 | tf_op jit(solution)/shard_map/all_to_all | solution.py:133
  56.7 0.6 fusion.106
  57.3 18.0 %all-to-all-done.1 = bf16[4,2,49152]{2,1,0:T(2,128)(2,1)S(1)} async-done(((bf16[4,2,49152]{2,1,0:T(2,128)(2,1)}), bf16[4,2,49152]{2,1,0:T(2,128)(2,1)S(1)}, u32[]{:S(2)}, u32[]{:S(2)}) %all-to-all-start.1) | async-done | bytes 786464 | tf_op jit(solution)/shard_map/all_to_all | solution.py:133
  75.3 4.2 %reshape.141 = bf16[2048,6,32]{2,1,0:T(8,128)(2,1)} reshape(bf16[4,2,49152]{2,1,0:T(2,128)(2,1)S(1)} %all-to-all-done.1) | data formatting | bytes 1572864
  79.5 4.5 %copy.39 = bf16[6,32,4,512]{3,2,1,0:T(4,128)(2,1)S(1)} copy(bf16[6,32,4,512]{1,0,3,2:T(8,128)(2,1)} %bitcast.80) | data formatting | bytes 1572864 | tf_op jit(solution)/shard_map/all_to_all | solution.py:133
  84.2 1.0 convolution_convert_fusion
  85.3 2.0 %collective-permute-start.1 = (bf16[1,6,32,512]{3,2,0,1:T(8,128)(2,1)S(1)}, bf16[1,6,32,512]{3,2,0,1:T(8,128)(2,1)S(1)}, u32[]{:S(2)}, u32[]{:S(2)}) collective-permute-start(bf16[1,6,32,512]{3,2,0,1:T(8,128)(2,1)S(1)} %get-tuple-element.125), channel_id=1, source_target_pairs={{0,8},{4,12},{8,0},{12,4},{1,9},{5,13},{9,1},{13,5},{2,10},{6,14},... | collective-permute-start | bytes 589832 | tf_op jit(solution)/shard_map/ppermute | solution.py:36
  87.3 1.8 %collective-permute-start.2 = (bf16[1,6,32,512]{3,2,0,1:T(8,128)(2,1)S(1)}, bf16[1,6,32,512]{3,2,0,1:T(8,128)(2,1)S(1)}, u32[]{:S(2)}, u32[]{:S(2)}) collective-permute-start(bf16[1,6,32,512]{3,2,0,1:T(8,128)(2,1)S(1)} %get-tuple-element.124), channel_id=1, source_target_pairs={{0,12},{4,0},{8,4},{12,8},{1,13},{5,1},{9,5},{13,9},{2,14},{6,2},{... | collective-permute-start | bytes 589832 | tf_op jit(solution)/shard_map/ppermute | solution.py:36
  89.1 5.9 %collective-permute-done = bf16[1,6,32,512]{3,2,0,1:T(8,128)(2,1)S(1)} collective-permute-done((bf16[1,6,32,512]{3,2,0,1:T(8,128)(2,1)S(1)}, bf16[1,6,32,512]{3,2,0,1:T(8,128)(2,1)S(1)}, u32[]{:S(2)}, u32[]{:S(2)}) %collective-permute-start) | collective-permute-done | bytes 196640 | tf_op jit(solution)/shard_map/ppermute | solution.py:36
  95.0 6.5 %collective-permute-done.1 = bf16[1,6,32,512]{3,2,0,1:T(8,128)(2,1)S(1)} collective-permute-done((bf16[1,6,32,512]{3,2,0,1:T(8,128)(2,1)S(1)}, bf16[1,6,32,512]{3,2,0,1:T(8,128)(2,1)S(1)}, u32[]{:S(2)}, u32[]{:S(2)}) %collective-permute-start.1) | collective-permute-done | bytes 196640 | tf_op jit(solution)/shard_map/ppermute | solution.py:36
  101.6 0.6 copy.32
  102.2 0.3 reshape_reshape.3
  102.5 1.6 %collective-permute-start.4 = (bf16[6,32,16,128]{3,2,1,0:T(8,128)(2,1)S(1)}, bf16[6,32,16,128]{3,2,1,0:T(8,128)(2,1)S(1)}, u32[]{:S(2)}, u32[]{:S(2)}) collective-permute-start(bf16[6,32,16,128]{3,2,1,0:T(8,128)(2,1)S(1)} %reshape_reshape.3), channel_id=1, source_target_pairs={{2,0},{0,2},{3,1},{1,3},{6,4},{4,6},{7,5},{5,7},{10,8},{8,10},{11,... | collective-permute-start | bytes 2359304 | tf_op jit(solution)/shard_map/ppermute | solution.py:52
  104.1 0.5 collective-permute-start.3
  104.6 18.5 %collective-permute-done.4 = bf16[6,32,16,128]{3,2,1,0:T(8,128)(2,1)S(1)} collective-permute-done((bf16[6,32,16,128]{3,2,1,0:T(8,128)(2,1)S(1)}, bf16[6,32,16,128]{3,2,1,0:T(8,128)(2,1)S(1)}, u32[]{:S(2)}, u32[]{:S(2)}) %collective-permute-start.4) | collective-permute-done | bytes 786464 | tf_op jit(solution)/shard_map/ppermute | solution.py:52
  123.1 14.0 %collective-permute-done.3 = bf16[6,32,16,128]{3,2,1,0:T(8,128)(2,1)S(1)} collective-permute-done((bf16[6,32,16,128]{3,2,1,0:T(8,128)(2,1)S(1)}, bf16[6,32,16,128]{3,2,1,0:T(8,128)(2,1)S(1)}, u32[]{:S(2)}, u32[]{:S(2)}) %collective-permute-start.3) | collective-permute-done | bytes 786464 | tf_op jit(solution)/shard_map/ppermute | solution.py:51
  137.0 1.1 fusion.35
  138.1 0.4 fusion.122
  138.5 0.6 copy.34
  139.2 0.6 copy.33
  139.8 0.5 collective-permute-start.5
  140.3 0.5 collective-permute-done.6
  140.9 0.6 copy.36
  141.7 0.6 copy.35
  142.3 2.6 %add_convert_fusion = bf16[6,32,16,128]{3,2,1,0:T(8,128)(2,1)} fusion(bf16[6,32,16,128]{3,2,1,0:T(8,128)(2,1)S(1)} %copy-done.1, bf16[6,32,16,16]{3,2,1,0:T(8,128)(2,1)S(1)} %copy.36, bf16[6,32,16,128]{3,2,1,0:T(8,128)(2,1)S(1)} %fusion.35, bf16[6,32,16,16]{3,2,1,0:T(8,128)(2,1)S(1)} %copy.35, f32[]{:T(128)} %fusion.106), kind=kOutput, calls=%fused_computation.31 | convolution fusion | flops 130203648 | bytes 2555908 | tf_op jit(solution)/shard_map/cxyj,ij->cxyi/dot_general | solution.py:148
  (50 shorter events, 2.1 us)
Async XLA Ops:
  0.0 6.2 %copy-start = (s32[4096,1]{0,1:T(1,128)S(1)}, s32[4096,1]{0,1:T(1,128)}, u32[]{:S(2)}) copy-start(s32[4096,1]{0,1:T(1,128)} %param.8) | copy-start | bytes 49156
  19.0 13.8 %all-to-all-start = ((bf16[9,4,1536]{2,0,1:T(8,128)(2,1)}), bf16[9,4,1536]{2,0,1:T(8,128)(2,1)S(1)}, u32[]{:S(2)}, u32[]{:S(2)}) async-start(bf16[9,4,1536]{2,0,1:T(8,128)(2,1)} %copy.26), calls=%async_computation | async-start | bytes 393216 | tf_op jit(solution)/shard_map/all_to_all | solution.py:102
  53.1 22.2 %all-to-all-start.1 = ((bf16[4,2,49152]{2,1,0:T(2,128)(2,1)}), bf16[4,2,49152]{2,1,0:T(2,128)(2,1)S(1)}, u32[]{:S(2)}, u32[]{:S(2)}) async-start(bf16[4,2,49152]{2,1,0:T(2,128)(2,1)} %reshape.140), calls=%async_computation.1 | async-start | bytes 1572864 | tf_op jit(solution)/shard_map/all_to_all | solution.py:133
  85.2 9.8 %collective-permute-start = (bf16[1,6,32,512]{3,2,0,1:T(8,128)(2,1)S(1)}, bf16[1,6,32,512]{3,2,0,1:T(8,128)(2,1)S(1)}, u32[]{:S(2)}, u32[]{:S(2)}) collective-permute-start(bf16[1,6,32,512]{3,2,0,1:T(8,128)(2,1)S(1)} %get-tuple-element.126), channel_id=1, source_target_pairs={{0,4},{4,8},{8,12},{12,0},{1,5},{5,9},{9,13},{13,1},{2,6},{6,10},{... | collective-permute-start | bytes 589832 | tf_op jit(solution)/shard_map/ppermute | solution.py:36
  85.3 16.3 %collective-permute-start.1 = (bf16[1,6,32,512]{3,2,0,1:T(8,128)(2,1)S(1)}, bf16[1,6,32,512]{3,2,0,1:T(8,128)(2,1)S(1)}, u32[]{:S(2)}, u32[]{:S(2)}) collective-permute-start(bf16[1,6,32,512]{3,2,0,1:T(8,128)(2,1)S(1)} %get-tuple-element.125), channel_id=1, source_target_pairs={{0,8},{4,12},{8,0},{12,4},{1,9},{5,13},{9,1},{13,5},{2,10},{6,14},... | collective-permute-start | bytes 589832 | tf_op jit(solution)/shard_map/ppermute | solution.py:36
  87.3 14.3 %collective-permute-start.2 = (bf16[1,6,32,512]{3,2,0,1:T(8,128)(2,1)S(1)}, bf16[1,6,32,512]{3,2,0,1:T(8,128)(2,1)S(1)}, u32[]{:S(2)}, u32[]{:S(2)}) collective-permute-start(bf16[1,6,32,512]{3,2,0,1:T(8,128)(2,1)S(1)} %get-tuple-element.124), channel_id=1, source_target_pairs={{0,12},{4,0},{8,4},{12,8},{1,13},{5,1},{9,5},{13,9},{2,14},{6,2},{... | collective-permute-start | bytes 589832 | tf_op jit(solution)/shard_map/ppermute | solution.py:36
  102.5 20.5 %collective-permute-start.4 = (bf16[6,32,16,128]{3,2,1,0:T(8,128)(2,1)S(1)}, bf16[6,32,16,128]{3,2,1,0:T(8,128)(2,1)S(1)}, u32[]{:S(2)}, u32[]{:S(2)}) collective-permute-start(bf16[6,32,16,128]{3,2,1,0:T(8,128)(2,1)S(1)} %reshape_reshape.3), channel_id=1, source_target_pairs={{2,0},{0,2},{3,1},{1,3},{6,4},{4,6},{7,5},{5,7},{10,8},{8,10},{11,... | collective-permute-start | bytes 2359304 | tf_op jit(solution)/shard_map/ppermute | solution.py:52
  104.1 33.0 %collective-permute-start.3 = (bf16[6,32,16,128]{3,2,1,0:T(8,128)(2,1)S(1)}, bf16[6,32,16,128]{3,2,1,0:T(8,128)(2,1)S(1)}, u32[]{:S(2)}, u32[]{:S(2)}) collective-permute-start(bf16[6,32,16,128]{3,2,1,0:T(8,128)(2,1)S(1)} %reshape_reshape.3), channel_id=1, source_target_pairs={{0,2},{2,0},{1,3},{3,1},{4,6},{6,4},{5,7},{7,5},{8,10},{10,8},{9,1... | collective-permute-start | bytes 2359304 | tf_op jit(solution)/shard_map/ppermute | solution.py:51
  139.1 1.8 %collective-permute-start.6 = (bf16[6,32,16,16]{1,3,2,0:T(8,128)(2,1)S(1)}, bf16[6,32,16,16]{1,3,2,0:T(8,128)(2,1)S(1)}, u32[]{:S(2)}, u32[]{:S(2)}) collective-permute-start(bf16[6,32,16,16]{1,3,2,0:T(8,128)(2,1)S(1)} %copy.34), channel_id=1, source_target_pairs={{1,0},{0,1},{3,2},{2,3},{5,4},{4,5},{7,6},{6,7},{9,8},{8,9},{11,10... | collective-permute-start | bytes 294920 | tf_op jit(solution)/shard_map/ppermute | solution.py:52
  139.2 3.2 %copy-start.1 = (bf16[6,32,16,128]{3,2,1,0:T(8,128)(2,1)S(1)}, bf16[6,32,16,128]{3,2,1,0:T(8,128)(2,1)}, u32[]{:S(2)}) copy-start(bf16[6,32,16,128]{3,2,1,0:T(8,128)(2,1)} %param.11) | copy-start | bytes 2359300
  139.8 1.9 %collective-permute-start.5 = (bf16[6,32,16,16]{1,3,2,0:T(8,128)(2,1)S(1)}, bf16[6,32,16,16]{1,3,2,0:T(8,128)(2,1)S(1)}, u32[]{:S(2)}, u32[]{:S(2)}) collective-permute-start(bf16[6,32,16,16]{1,3,2,0:T(8,128)(2,1)S(1)} %copy.33), channel_id=1, source_target_pairs={{0,1},{1,0},{2,3},{3,2},{4,5},{5,4},{6,7},{7,6},{8,9},{9,8},{10,11... | collective-permute-start | bytes 294920 | tf_op jit(solution)/shard_map/ppermute | solution.py:51
